TPU v7x, 32 devices: a whole 2x2x4 slice. The times are simulated.
32 devices in a mesh: dp: 4 (over x, core), ctx: 8 (over z, y).
Axes of the slice: x: 2, y: 2, z: 4, core: 2. Of those that a mesh axis runs over, the one named last changes fastest.
Arguments:
- hidden: bfloat16 [4, 2048, 8192], P('dp', 'ctx')
- norm_gain: bfloat16 [8192], replicated, may hold values from 0.5 to 2
- queries: bfloat16 [4, 2048, 4096], P('dp', 'ctx')
- key_weight: bfloat16 [8192, 512], P('dp'), may hold values from -0.0625 to 0.0625
- value_weight: bfloat16 [8192, 512], P('dp'), may hold values from -0.0625 to 0.0625
- block_lists: int32 [4, 32, 16, 12], P('dp', 'ctx'), may hold values from 0 to 15, as said below
- block_counts: int32 [4, 32, 16], P('dp', 'ctx'), may hold values from 1 to 12, as said below
Outputs:
- attended: bfloat16 [4, 2048, 4096], P('dp', 'ctx')
Inputs may be any that keep to these rules, and one draw needn't show every extreme that they name: `block_lists`: for each spreadsheet, head and query block i, the first block_counts entries are distinct key blocks: the first is i, each later one is smaller than the one before (the blocks of i's ancestors in that head's header tree, nearest first); entries past the count equal i and are to be ignored. `block_counts`: every spreadsheet has a query block with 12 listed blocks; the counts differ much from head to head.
All inputs are finite; a program needn't handle non-finite values.
Results may differ from a plain program's by a relative error of at most 0.0078.
Values may be sent and summed in bfloat16 or wider, within the bound.
A program may use at most 128 MiB of HBM per device.

v0:
```python
import math

import jax
import jax.numpy as jnp
from jax import lax
from jax.sharding import PartitionSpec as P

KVH = 4
HD = 128
BLK = 128
MAXB = 12


def on_device(hidden, norm_gain, queries, key_weight, value_weight, block_lists, block_counts):
    upcast = hidden[0].astype(jnp.float32)
    mean_square = jnp.mean(upcast * upcast, axis=-1, keepdims=True)
    normed = (upcast * lax.rsqrt(mean_square + 1e-05) * norm_gain.astype(jnp.float32)).astype(
        jnp.bfloat16
    )
    local_rows = normed.shape[0]
    key_part = jnp.einsum(
        "df,td->ft",
        lax.all_gather(key_weight, "dp", axis=0, tiled=True),
        normed,
        preferred_element_type=jnp.float32,
    )
    value_part = jnp.einsum(
        "df,td->ft",
        lax.all_gather(value_weight, "dp", axis=0, tiled=True),
        normed,
        preferred_element_type=jnp.float32,
    )
    paired = jnp.stack([key_part, value_part]).astype(jnp.bfloat16)
    ctx_size = lax.axis_size("ctx")
    copies_per_head = ctx_size // KVH
    widened = jnp.broadcast_to(
        paired.reshape(2, KVH, 1, HD, local_rows), (2, KVH, copies_per_head, HD, local_rows)
    )
    widened = widened.reshape(2, ctx_size * HD, local_rows)
    head_pair = lax.all_to_all(widened, "ctx", split_axis=1, concat_axis=2, tiled=True)
    head_queries = lax.all_to_all(queries[0], "ctx", split_axis=1, concat_axis=0, tiled=True)
    sequence_rows = head_queries.shape[0]
    heads_here = head_queries.shape[1] // HD
    block_total = sequence_rows // BLK
    query_blocks = head_queries.reshape(block_total, BLK, heads_here, HD)
    key_blocks = head_pair[0].reshape(HD, block_total, BLK)
    value_blocks = head_pair[1].reshape(HD, block_total, BLK)
    lists_here = block_lists[0]
    counts_here = block_counts[0]
    score_scale = HD ** (-0.5)
    within_rows = jnp.arange(BLK)[None, :, None, None]
    within_cols = jnp.arange(BLK)[None, None, None, :]
    block_ids = jnp.arange(block_total, dtype=jnp.int32)
    group_blocks = math.gcd(block_total, 4)

    def one_group(group_index):
        first_block = group_index * group_blocks
        query_group = lax.dynamic_slice_in_dim(query_blocks, first_block, group_blocks, 0)
        lists_group = lax.dynamic_slice_in_dim(lists_here, first_block, group_blocks, 1)
        counts_group = lax.dynamic_slice_in_dim(counts_here, first_block, group_blocks, 1)

        def slot_scores(slot_index):
            chosen = lax.dynamic_index_in_dim(lists_group, slot_index, axis=2, keepdims=False)
            selector = (chosen[..., None] == block_ids).astype(jnp.bfloat16)
            picked = jnp.einsum(
                "hnb,dbk->dhnk", selector, key_blocks, preferred_element_type=jnp.float32
            ).astype(jnp.bfloat16)
            scores = (
                jnp.einsum(
                    "nthd,dhnk->nthk", query_group, picked, preferred_element_type=jnp.float32
                )
                * score_scale
            )
            live_slots = (slot_index < counts_group).T[:, None, :, None]
            allowed = live_slots & ((slot_index > 0) | (within_cols <= within_rows))
            return jnp.where(allowed, scores, -jnp.inf)

        masked = jnp.stack([slot_scores(slot_index) for slot_index in range(MAXB)])
        row_peak = jnp.max(masked, axis=(0, 4))
        exponent = jnp.exp(masked - row_peak[None, ..., None])
        denominator = jnp.sum(exponent, axis=(0, 4))
        value_selector = (lists_group[..., None] == block_ids).astype(jnp.bfloat16)
        picked_values = jnp.einsum(
            "hnsb,dbk->dhnsk", value_selector, value_blocks, preferred_element_type=jnp.float32
        ).astype(jnp.bfloat16)
        weighted = jnp.einsum(
            "snthk,dhnsk->nthd",
            exponent.astype(jnp.bfloat16),
            picked_values,
            preferred_element_type=jnp.float32,
        )
        return (weighted / denominator[..., None]).astype(jnp.bfloat16)

    grouped = lax.map(one_group, jnp.arange(block_total // group_blocks))
    attended_heads = grouped.reshape(sequence_rows, heads_here * HD)
    restored = lax.all_to_all(attended_heads, "ctx", split_axis=0, concat_axis=1, tiled=True)
    return restored[None]


def solution(mesh):
    return jax.shard_map(
        on_device,
        mesh=mesh,
        in_specs=(
            P("dp", "ctx", None),
            P(),
            P("dp", "ctx", None),
            P("dp", None),
            P("dp", None),
            P("dp", "ctx", None, None),
            P("dp", "ctx", None),
        ),
        out_specs=P("dp", "ctx", None),
        check_vma=False,
    )
```

profile of v0, /device:TPU:28, one launch (start us, length us, event | category | flops | bytes accessed | tf_op | source)
XLA Modules:
  0.0 378.2 jit_solution(17061625898404295067)
XLA Ops:
  6.5 0.7 all-gather.3.cloned.1.call-update
  7.3 0.7 all-gather.5.cloned.1.call-update
  8.0 4.1 %copy.64 = bf16[1,256,4096]{1,2,0:T(8,128)(2,1)} copy(bf16[1,256,4096]{2,1,0:T(8,128)(2,1)} %param.11) | data formatting | bytes 4194304 | tf_op args[2]
  12.1 6.0 %all-to-all-start.1 = ((bf16[256,8,512]{0,2,1:T(8,128)(2,1)}), bf16[256,8,512]{0,2,1:T(8,128)(2,1)S(1)}, u32[]{:S(2)}, u32[]{:S(2)}) async-start(bf16[256,8,512]{0,2,1:T(8,128)(2,1)} %bitcast.476), calls=%async_computation.1 | async-start | bytes 4194304 | tf_op jit(solution)/shard_map/all_to_all | solution.py:41
  18.1 3.7 fusion.126
  21.8 46.4 %all-gather.3.cloned.1.call-done = bf16[8192,512]{1,0:T(8,128)(2,1)} async-done(((bf16[2048,512]{1,0:T(8,128)(2,1)}), bf16[8192,512]{1,0:T(8,128)(2,1)}) %all-gather.3.cloned.1.call-update) | async-done | bytes 8388624 | tf_op jit(solution)/shard_map/all_gather | solution.py:23
  68.2 7.0 %fusion.131 = bf16[512,256]{0,1:T(8,128)(2,1)S(1)} fusion(bf16[8192,512]{1,0:T(8,128)(2,1)} %all-gather.3.cloned.1.call-done, bf16[1,256,8192]{2,1,0:T(8,128)(2,1)} %param.9, f32[8192]{0:T(1024)S(1)} %convert_element_type.116, f32[256]{0:T(256)S(1)} %add_rsqrt_fusion), kind=kOutput, calls=%fused_computation.198 | convolution fusion | flops 2156003328 | bytes 12878848 | tf_op jit(solution)/shard_map/df,td->ft/dot_general | solution.py:21
  75.3 52.8 %all-gather.5.cloned.1.call-done = bf16[8192,512]{1,0:T(8,128)(2,1)} async-done(((bf16[2048,512]{1,0:T(8,128)(2,1)}), bf16[8192,512]{1,0:T(8,128)(2,1)}) %all-gather.5.cloned.1.call-update) | async-done | bytes 8388624 | tf_op jit(solution)/shard_map/all_gather | solution.py:29
  128.1 7.0 %fusion.134 = bf16[512,256]{0,1:T(8,128)(2,1)S(1)} fusion(bf16[8192,512]{1,0:T(8,128)(2,1)} %all-gather.5.cloned.1.call-done, bf16[1,256,8192]{2,1,0:T(8,128)(2,1)} %param.9, f32[8192]{0:T(1024)S(1)} %convert_element_type.116, f32[256]{0:T(256)S(1)} %add_rsqrt_fusion), kind=kOutput, calls=%fused_computation.199 | convolution fusion | flops 2156003328 | bytes 12878848 | tf_op jit(solution)/shard_map/df,td->ft/dot_general | solution.py:27
  135.5 0.8 copy.60
  136.4 1.5 broadcast_in_dim.27
  137.9 6.0 %all-to-all-start = ((bf16[2,1024,256]{2,0,1:T(2,128)(2,1)}), bf16[2,1024,256]{2,0,1:T(2,128)(2,1)S(1)}, u32[]{:S(2)}, u32[]{:S(2)}) async-start(bf16[2,1024,256]{2,0,1:T(2,128)(2,1)} %bitcast.479), calls=%async_computation | async-start | bytes 2097152 | tf_op jit(solution)/shard_map/all_to_all | solution.py:40
  143.9 2.5 copy.65
  146.4 4.1 %reshape.141 = bf16[16,128,4,128]{1,0,3,2:T(8,128)(2,1)} reshape(bf16[8,256,512]{1,0,2:T(8,128)(2,1)} %copy.65) | data formatting | bytes 4194304 | tf_op jit(solution)/shard_map/reshape | solution.py:45
  150.5 17.2 %all-to-all-done = bf16[2,1024,256]{2,0,1:T(2,128)(2,1)S(1)} async-done(((bf16[2,1024,256]{2,0,1:T(2,128)(2,1)}), bf16[2,1024,256]{2,0,1:T(2,128)(2,1)S(1)}, u32[]{:S(2)}, u32[]{:S(2)}) %all-to-all-start) | async-done | bytes 1048608 | tf_op jit(solution)/shard_map/all_to_all | solution.py:40
  169.4 141.5 %while.12 = (s32[]{:T(128)}, bf16[4,4,128,4,128]{4,3,2,1,0:T(4,128)(2,1)}, s32[4]{0:T(128)S(1)}, s32[4,16,12]{1,0,2:T(4,128)S(1)}, bf16[128,16,128]{2,1,0:T(8,12...) while((s32[]{:T(128)}, ...), condition=%wide.region_15.16_spmd.clone.clone, body=%wide.region_1.15_spmd.clone.clone.sunk | while | flops 1837910272 | bytes 181679120 | solution.py:94
  169.6 0.7 dynamic_slice.92
  171.4 1.5 constant_dynamic-slice_fusion.18
  184.1 4.6 %copy-done = f32[12,4,128,4,128]{2,4,3,1,0:T(8,128)} copy-done((f32[12,4,128,4,128]{2,4,3,1,0:T(8,128)}, f32[12,4,128,4,128]{2,4,3,1,0:T(8,128)S(1)}, u32[]{:S(2)}) %copy-start) | copy-done | bytes 12582936 | tf_op jit(solution)/shard_map/while
  189.4 9.4 %fusion.260 = (f32[4,128,4]{1,2,0:T(4,128)S(1)}, bf16[12,4,128,4,128]{2,4,3,1,0:T(8,128)(2,1)}) fusion(f32[12,4,128,4,128]{2,4,3,1,0:T(8,128)} %copy-done, f32[4,128,4]{1,2,0:T(4,128)S(1)} %bitcast.494), kind=kLoop, calls=%fused_computation.4.clone.1 | loop fusion | flops 9435136 | bytes 18890752 | tf_op jit(solution)/shard_map/while/body/eval_jaxpr/reduce_sum | solution.py:81
  199.0 2.4 convert_bitcast_fusion.2
  201.8 1.9 fusion.261
  204.0 1.0 constant_dynamic-update-slice_fusion.2
  204.9 0.7 dynamic_slice.92
  206.8 1.5 constant_dynamic-slice_fusion.18
  219.4 4.6 %copy-done = f32[12,4,128,4,128]{2,4,3,1,0:T(8,128)} copy-done((f32[12,4,128,4,128]{2,4,3,1,0:T(8,128)}, f32[12,4,128,4,128]{2,4,3,1,0:T(8,128)S(1)}, u32[]{:S(2)}) %copy-start) | copy-done | bytes 12582936 | tf_op jit(solution)/shard_map/while
  224.8 9.4 %fusion.260 = (f32[4,128,4]{1,2,0:T(4,128)S(1)}, bf16[12,4,128,4,128]{2,4,3,1,0:T(8,128)(2,1)}) fusion(f32[12,4,128,4,128]{2,4,3,1,0:T(8,128)} %copy-done, f32[4,128,4]{1,2,0:T(4,128)S(1)} %bitcast.494), kind=kLoop, calls=%fused_computation.4.clone.1 | loop fusion | flops 9435136 | bytes 18890752 | tf_op jit(solution)/shard_map/while/body/eval_jaxpr/reduce_sum | solution.py:81
  234.3 2.4 convert_bitcast_fusion.2
  237.1 1.9 fusion.261
  239.3 1.0 constant_dynamic-update-slice_fusion.2
  240.3 0.7 dynamic_slice.92
  242.1 1.5 constant_dynamic-slice_fusion.18
  254.8 4.6 %copy-done = f32[12,4,128,4,128]{2,4,3,1,0:T(8,128)} copy-done((f32[12,4,128,4,128]{2,4,3,1,0:T(8,128)}, f32[12,4,128,4,128]{2,4,3,1,0:T(8,128)S(1)}, u32[]{:S(2)}) %copy-start) | copy-done | bytes 12582936 | tf_op jit(solution)/shard_map/while
  260.1 9.4 %fusion.260 = (f32[4,128,4]{1,2,0:T(4,128)S(1)}, bf16[12,4,128,4,128]{2,4,3,1,0:T(8,128)(2,1)}) fusion(f32[12,4,128,4,128]{2,4,3,1,0:T(8,128)} %copy-done, f32[4,128,4]{1,2,0:T(4,128)S(1)} %bitcast.494), kind=kLoop, calls=%fused_computation.4.clone.1 | loop fusion | flops 9435136 | bytes 18890752 | tf_op jit(solution)/shard_map/while/body/eval_jaxpr/reduce_sum | solution.py:81
  269.6 2.4 convert_bitcast_fusion.2
  272.4 1.9 fusion.261
  274.6 1.0 constant_dynamic-update-slice_fusion.2
  275.6 0.7 dynamic_slice.92
  277.4 1.5 constant_dynamic-slice_fusion.18
  290.1 4.6 %copy-done = f32[12,4,128,4,128]{2,4,3,1,0:T(8,128)} copy-done((f32[12,4,128,4,128]{2,4,3,1,0:T(8,128)}, f32[12,4,128,4,128]{2,4,3,1,0:T(8,128)S(1)}, u32[]{:S(2)}) %copy-start) | copy-done | bytes 12582936 | tf_op jit(solution)/shard_map/while
  295.4 9.4 %fusion.260 = (f32[4,128,4]{1,2,0:T(4,128)S(1)}, bf16[12,4,128,4,128]{2,4,3,1,0:T(8,128)(2,1)}) fusion(f32[12,4,128,4,128]{2,4,3,1,0:T(8,128)} %copy-done, f32[4,128,4]{1,2,0:T(4,128)S(1)} %bitcast.494), kind=kLoop, calls=%fused_computation.4.clone.1 | loop fusion | flops 9435136 | bytes 18890752 | tf_op jit(solution)/shard_map/while/body/eval_jaxpr/reduce_sum | solution.py:81
  305.0 2.4 convert_bitcast_fusion.2
  307.8 1.9 fusion.261
  309.9 1.0 constant_dynamic-update-slice_fusion.2
  310.9 2.7 all_to_all.41
  313.7 51.9 %all_to_all.47 = bf16[8,256,512]{2,1,0:T(8,128)(2,1)} all-to-all(bf16[8,256,512]{2,1,0:T(8,128)(2,1)S(1)} %all_to_all.41), channel_id=1, replica_groups=mesh['dp'=4,'ctx'=8] {'ctx'}, dimensions={0} | all-to-all | bytes 4194304 | tf_op jit(solution)/shard_map/all_to_all | solution.py:96
  365.6 2.8 copy.71
  368.5 2.9 copy.72
  (198 shorter events, 54.8 us)
Async XLA Ops:
  6.5 11.5 %copy-start.4 = (bf16[8192]{0:T(1024)(128)(2,1)S(1)}, bf16[8192]{0:T(1024)(128)(2,1)}, u32[]{:S(2)}) copy-start(bf16[8192]{0:T(1024)(128)(2,1)} %param.10) | copy-start | bytes 49156
  6.5 61.6 %all-gather.3.cloned.1.call-start = ((), (), s32[]{:S(2)}) async-start(), calls=%async_computation.3 | async-start | bytes 10485760 | tf_op jit(solution)/shard_map/all_gather | solution.py:23
  7.3 120.8 %all-gather.5.cloned.1.call-start = ((), (), s32[]{:S(2)}) async-start(), calls=%async_computation.4 | async-start | bytes 10485760 | tf_op jit(solution)/shard_map/all_gather | solution.py:29
  12.1 124.3 %all-to-all-start.1 = ((bf16[256,8,512]{0,2,1:T(8,128)(2,1)}), bf16[256,8,512]{0,2,1:T(8,128)(2,1)S(1)}, u32[]{:S(2)}, u32[]{:S(2)}) async-start(bf16[256,8,512]{0,2,1:T(8,128)(2,1)} %bitcast.476), calls=%async_computation.1 | async-start | bytes 4194304 | tf_op jit(solution)/shard_map/all_to_all | solution.py:41
  137.9 29.8 %all-to-all-start = ((bf16[2,1024,256]{2,0,1:T(2,128)(2,1)}), bf16[2,1024,256]{2,0,1:T(2,128)(2,1)S(1)}, u32[]{:S(2)}, u32[]{:S(2)}) async-start(bf16[2,1024,256]{2,0,1:T(2,128)(2,1)} %bitcast.479), calls=%async_computation | async-start | bytes 2097152 | tf_op jit(solution)/shard_map/all_to_all | solution.py:40
  143.9 25.5 %copy-start.2 = (s32[1,4,16,12]{2,1,3,0:T(4,128)S(1)}, s32[1,4,16,12]{2,1,3,0:T(4,128)}, u32[]{:S(2)}) copy-start(s32[1,4,16,12]{2,1,3,0:T(4,128)} %param.14) | copy-start | bytes 9220
  143.9 25.5 %copy-start.3 = (s32[1,4,16]{2,1,0:T(4,128)S(1)}, s32[1,4,16]{2,1,0:T(4,128)}, u32[]{:S(2)}) copy-start(s32[1,4,16]{2,1,0:T(4,128)} %param.15) | copy-start | bytes 772
  184.1 4.6 %copy-start = (f32[12,4,128,4,128]{2,4,3,1,0:T(8,128)}, f32[12,4,128,4,128]{2,4,3,1,0:T(8,128)S(1)}, u32[]{:S(2)}) copy-start(f32[12,4,128,4,128]{2,4,3,1,0:T(8,128)S(1)} %get-tuple-element.410) | copy-start | bytes 37748740 | tf_op jit(solution)/shard_map/while
  199.0 2.8 copy-start.1
  219.4 4.6 %copy-start = (f32[12,4,128,4,128]{2,4,3,1,0:T(8,128)}, f32[12,4,128,4,128]{2,4,3,1,0:T(8,128)S(1)}, u32[]{:S(2)}) copy-start(f32[12,4,128,4,128]{2,4,3,1,0:T(8,128)S(1)} %get-tuple-element.410) | copy-start | bytes 37748740 | tf_op jit(solution)/shard_map/while
  234.3 2.8 copy-start.1
  254.8 4.6 %copy-start = (f32[12,4,128,4,128]{2,4,3,1,0:T(8,128)}, f32[12,4,128,4,128]{2,4,3,1,0:T(8,128)S(1)}, u32[]{:S(2)}) copy-start(f32[12,4,128,4,128]{2,4,3,1,0:T(8,128)S(1)} %get-tuple-element.410) | copy-start | bytes 37748740 | tf_op jit(solution)/shard_map/while
  269.6 2.8 copy-start.1
  290.1 4.6 %copy-start = (f32[12,4,128,4,128]{2,4,3,1,0:T(8,128)}, f32[12,4,128,4,128]{2,4,3,1,0:T(8,128)S(1)}, u32[]{:S(2)}) copy-start(f32[12,4,128,4,128]{2,4,3,1,0:T(8,128)S(1)} %get-tuple-element.410) | copy-start | bytes 37748740 | tf_op jit(solution)/shard_map/while
  305.0 2.8 copy-start.1
Sparse Core Ops, SparseCore 0:
  8.9 59.2 all-gather.2
  69.7 58.2 all-gather.4
where the time goes:
time: 383 us; the launch traced here: 378 us
  waiting for transfers between devices  118 us (31%)
  matrix products  72.8 us (19%)
  local copies, waits for them, and re-layouts  60.4 us (16%)
  blocking collectives  51.9 us (14%)
  other arithmetic  46.1 us (12%)
  between operations  13.5 us (4%)
  starting transfers between devices  12 us (3%)
    all_gather x1, waiting for transfers between devices, on_device(): lax.all_gather(value_weight, 'dp', axis=0, tiled=True)  52.8 us
    all_to_all x1, blocking collectives, on_device(): lax.all_to_all(attended_heads, 'ctx', split_axis=0, concat_axis=1, tiled=...  51.9 us
    all_gather x1, waiting for transfers between devices, on_device(): lax.all_gather(key_weight, 'dp', axis=0, tiled=True)  46.4 us
    reduce_sum x4, other arithmetic, one_group(): denominator = jnp.sum(exponent, axis=(0, 4))  37.5 us
    dot_general x48, matrix products, slot_scores(): jnp.einsum('nthd,dhnk->nthk', query_group, picked, preferred_element_type...  24.5 us
    while x16, local copies, waits for them, and re-layouts  19.9 us
    all_to_all x1, waiting for transfers between devices, on_device(): lax.all_to_all(widened, 'ctx', split_axis=1, concat_axis=2, tiled=True)  17.2 us
    dot_general x48, matrix products, slot_scores(): jnp.einsum('hnb,dbk->dhnk', selector, key_blocks, preferred_element_type=...  17.2 us
  transfers between devices with their start and end apart: 4, of which 3 were waited for; matrix products, arithmetic and copies ran while one was open for 8% of the time, Pallas kernels for 0%

commit v1 on v0

v1 whole, which is shorter than its diff:
```python
import functools

import jax
import jax.numpy as jnp
from jax import lax
from jax.experimental import pallas as pl
from jax.experimental.pallas import tpu as pltpu
from jax.sharding import PartitionSpec as P

KVH = 4
HD = 128
BLK = 128
MAXB = 12
LOG2E = 1.4426950408889634
BUCKETS = (2, 4, 6, 8, 10, 12)


def attention_kernel(heads, local_blocks, lists_ref, queries_ref, pairs_ref, out_ref):
    group = heads // KVH
    width = MAXB + 1
    factor = LOG2E * HD ** (-0.5)

    def one(index, carry):
        block = index // heads
        head = lax.rem(index, heads)
        kv = head // group
        base = (head * local_blocks + block) * width
        count = lists_ref[base + MAXB]
        rows = pl.ds(pl.multiple_of(block * BLK, BLK), BLK)
        columns = pl.ds(pl.multiple_of(head * HD, HD), HD)
        key_columns = pl.ds(pl.multiple_of(kv * HD, HD), HD)
        value_columns = pl.ds(pl.multiple_of((KVH + kv) * HD, HD), HD)

        def attend(slots):
            query = queries_ref[rows, columns]
            places = [
                pl.ds(pl.multiple_of(lists_ref[base + s] * BLK, BLK), BLK) for s in range(slots)
            ]
            keys = jnp.concatenate([pairs_ref[place, key_columns] for place in places], axis=0)
            scores = lax.dot_general(
                query, keys, (((1,), (1,)), ((), ())), preferred_element_type=jnp.float32
            )
            tiles = [scores[:, s * BLK : (s + 1) * BLK] for s in range(slots)]
            row = lax.broadcasted_iota(jnp.int32, (BLK, BLK), 0)
            column = lax.broadcasted_iota(jnp.int32, (BLK, BLK), 1)
            tiles[0] = jnp.where(column <= row, tiles[0], -jnp.inf)
            for s in range(max(1, slots - 1), slots):
                tiles[s] = jnp.where(s < count, tiles[s], -jnp.inf)
            peak = functools.reduce(jnp.maximum, tiles)
            peak = jnp.max(peak, axis=1, keepdims=True)
            tiles = [jnp.exp2((tile - peak) * factor) for tile in tiles]
            total = jnp.sum(functools.reduce(jnp.add, tiles), axis=1, keepdims=True)
            weights = jnp.concatenate([tile.astype(jnp.bfloat16) for tile in tiles], axis=1)
            values = jnp.concatenate([pairs_ref[place, value_columns] for place in places], axis=0)
            attended = jnp.dot(weights, values, preferred_element_type=jnp.float32)
            out_ref[rows, columns] = (attended / total).astype(jnp.bfloat16)

        below = 0
        for slots in BUCKETS:

            @pl.when((count > below) & (count <= slots))
            def _(slots=slots):
                attend(slots)

            below = slots
        return carry

    lax.fori_loop(0, heads * local_blocks, one, 0)


def attention(lists, queries, pairs, heads, local_blocks):
    return pl.pallas_call(
        functools.partial(attention_kernel, heads, local_blocks),
        out_shape=jax.ShapeDtypeStruct(queries.shape, jnp.bfloat16),
        in_specs=[
            pl.BlockSpec(memory_space=pltpu.SMEM),
            pl.BlockSpec(memory_space=pltpu.VMEM),
            pl.BlockSpec(memory_space=pltpu.VMEM),
        ],
        out_specs=pl.BlockSpec(memory_space=pltpu.VMEM),
        compiler_params=pltpu.CompilerParams(vmem_limit_bytes=48 * 2**20),
    )(lists, queries, pairs)


def on_device(hidden, norm_gain, queries, key_weight, value_weight, block_lists, block_counts):
    tables = jnp.concatenate([block_lists[0], block_counts[0][..., None]], axis=-1)
    tables = lax.all_to_all(tables, "ctx", split_axis=1, concat_axis=0, tiled=True)
    heads, local_blocks, _ = tables.shape
    upcast = hidden[0].astype(jnp.float32)
    mean_square = jnp.mean(upcast * upcast, axis=-1, keepdims=True)
    normed = (upcast * lax.rsqrt(mean_square + 1e-05) * norm_gain.astype(jnp.float32)).astype(
        jnp.bfloat16
    )
    key_all = lax.all_gather(key_weight, "dp", axis=0, tiled=True)
    value_all = lax.all_gather(value_weight, "dp", axis=0, tiled=True)
    keys = jnp.dot(normed, key_all, preferred_element_type=jnp.float32).astype(jnp.bfloat16)
    values = jnp.dot(normed, value_all, preferred_element_type=jnp.float32).astype(jnp.bfloat16)
    pairs = lax.all_gather(jnp.concatenate([keys, values], axis=1), "ctx", axis=0, tiled=True)
    return attention(tables.reshape(-1), queries[0], pairs, heads, local_blocks)[None]


def solution(mesh):
    return jax.shard_map(
        on_device,
        mesh=mesh,
        in_specs=(
            P("dp", "ctx", None),
            P(),
            P("dp", "ctx", None),
            P("dp", None),
            P("dp", None),
            P("dp", "ctx", None, None),
            P("dp", "ctx", None),
        ),
        out_specs=P("dp", "ctx", None),
        check_vma=False,
    )
```

time: 383 us -> 256 us (0.67)
  local copies, waits for them, and re-layouts: 60.4 us -> 0.39 us
  matrix products: 72.8 us -> 14.1 us
  waiting for transfers between devices: 118 us -> 172 us
  blocking collectives: 51.9 us -> 8.45 us
  other arithmetic: 46.1 us -> 4.78 us
  Pallas kernels: 0 us -> 40.1 us
  starting transfers between devices: 12 us -> 0.08 us
    all_gather x2 -> x3, waiting for transfers between devices: 99.1 us -> 171 us  [the longest x1 62 us: on_device(): lax.all_gather(jnp.concatenate([keys, values], axis=1), 'ctx', axis=0, ti...]
    dot_general x106 -> x2, matrix products: 72.8 us -> 14.1 us  [the longest x1 7.04 us: on_device(): jnp.dot(normed, value_all, preferred_element_type=jnp.float32)]
    all_to_all x1, blocking collectives: 51.9 us -> 8.45 us  [on_device(): lax.all_to_all(tables, 'ctx', split_axis=1, concat_axis=0, tiled=True)]
    pallas_call x0 -> x1, Pallas kernels: none -> 40.1 us  [attention(): pl.pallas_call(functools.partial(attention_kernel, heads, local_blocks),...]
    reduce_sum x4 -> x0, other arithmetic: 37.5 us -> none  [one_group(): denominator = jnp.sum(exponent, axis=(0, 4))]
    while x16 -> x0, local copies, waits for them, and re-layouts: 19.9 us -> none
    all_to_all x2 -> x0, waiting for transfers between devices: 17.2 us -> none  [the longest x1 17.2 us: on_device(): lax.all_to_all(widened, 'ctx', split_axis=1, concat_axis=2, tiled=True)]
    all_to_all x2 -> x0, starting transfers between devices: 12 us -> none  [the longest x1 6 us: on_device(): lax.all_to_all(queries[0], 'ctx', split_axis=1, concat_axis=0, tiled=True)]
  transfers between devices with their start and end apart: 4 -> 3, of which waited for: 3 -> 3; matrix products, arithmetic and copies ran while one was open for 8% -> 4% of each run, Pallas kernels for 0% -> 0%
where the time goes in v1:
time: 256 us; the launch traced here: 254 us
  waiting for transfers between devices  172 us (67%)
  Pallas kernels  40.1 us (16%)
  matrix products  14.1 us (6%)
  between operations  13.2 us (5%)
  blocking collectives  8.45 us (3%)
  other arithmetic  4.78 us (2%)
    all_gather x1, waiting for transfers between devices, on_device(): lax.all_gather(jnp.concatenate([keys, values], axis=1), 'ctx', axis=0, ti...  62 us
    all_gather x1, waiting for transfers between devices, on_device(): value_all = lax.all_gather(value_weight, 'dp', axis=0, tiled=True)  56.3 us
    all_gather x1, waiting for transfers between devices, on_device(): key_all = lax.all_gather(key_weight, 'dp', axis=0, tiled=True)  52.8 us
    pallas_call x1, Pallas kernels, attention(): pl.pallas_call(functools.partial(attention_kernel, heads, local_blocks),...  40.1 us
    all_to_all x1, blocking collectives, on_device(): lax.all_to_all(tables, 'ctx', split_axis=1, concat_axis=0, tiled=True)  8.45 us
    dot_general x1, matrix products, on_device(): jnp.dot(normed, value_all, preferred_element_type=jnp.float32)  7.04 us
    dot_general x1, matrix products, on_device(): jnp.dot(normed, key_all, preferred_element_type=jnp.float32)  7.04 us
  transfers between devices with their start and end apart: 3, of which 3 were waited for; matrix products, arithmetic and copies ran while one was open for 4% of the time, Pallas kernels for 0%

profile of v1, /device:TPU:28, one launch (start us, length us, event | category | flops | bytes accessed | tf_op | source)
XLA Modules:
  0.0 253.5 jit_solution(533160033002051409)
XLA Ops:
  6.5 0.0 all-gather.6.cloned.1.call-start
  6.5 0.7 all-gather.6.cloned.1.call-update
  7.3 0.0 all-gather.4.cloned.1.call-start
  7.3 0.7 all-gather.4.cloned.1.call-update
  8.0 0.0 all-gather.8.cloned.1.call-start
  8.1 0.7 convert_element_type.20
  8.8 3.1 %fusion = f32[256]{0:T(256)S(1)} fusion(bf16[1,256,8192]{2,1,0:T(8,128)(2,1)} %param.7), kind=kLoop, calls=%fused_computation.2 | loop fusion | flops 6291200 | bytes 4195328 | tf_op jit(solution)/shard_map/reduce_sum | solution.py:90
  11.9 56.3 %all-gather.6.cloned.1.call-done = bf16[8192,512]{1,0:T(8,128)(2,1)} async-done(((bf16[2048,512]{1,0:T(8,128)(2,1)}), bf16[8192,512]{1,0:T(8,128)(2,1)}) %all-gather.6.cloned.1.call-update) | async-done | bytes 8388624 | tf_op jit(solution)/shard_map/all_gather | solution.py:95
  68.2 7.0 %convolution_convert_fusion = bf16[256,512]{1,0:T(8,128)(2,1)S(1)} fusion(bf16[8192,512]{1,0:T(8,128)(2,1)} %all-gather.6.cloned.1.call-done, bf16[1,256,8192]{2,1,0:T(8,128)(2,1)} %param.7, f32[8192]{0:T(1024)S(1)} %convert_element_type.20, f32[256]{0:T(256)S(1)} %add_rsqrt_fusion), kind=kOutput, calls=%fused_computation.5 | convolution fusion | flops 2156003328 | bytes 12878848 | tf_op jit(solution)/shard_map/dot_general | solution.py:97
  75.2 0.0 copy-start.1
  75.2 0.0 copy-start.2
  75.2 0.0 copy-start
  75.2 52.8 %all-gather.4.cloned.1.call-done = bf16[8192,512]{1,0:T(8,128)(2,1)} async-done(((bf16[2048,512]{1,0:T(8,128)(2,1)}), bf16[8192,512]{1,0:T(8,128)(2,1)}) %all-gather.4.cloned.1.call-update) | async-done | bytes 8388624 | tf_op jit(solution)/shard_map/all_gather | solution.py:94
  128.0 7.0 %convolution_convert_fusion.1 = bf16[256,512]{1,0:T(8,128)(2,1)S(1)} fusion(bf16[8192,512]{1,0:T(8,128)(2,1)} %all-gather.4.cloned.1.call-done, bf16[1,256,8192]{2,1,0:T(8,128)(2,1)} %param.7, f32[8192]{0:T(1024)S(1)} %convert_element_type.20, f32[256]{0:T(256)S(1)} %add_rsqrt_fusion), kind=kOutput, calls=%fused_computation.6 | convolution fusion | flops 2156003328 | bytes 12878848 | tf_op jit(solution)/shard_map/dot_general | solution.py:96
  135.1 0.9 pad_maximum_fusion
  136.0 0.0 all-gather.8.cloned.1.call-update
  136.0 0.0 copy-done.1
  136.0 0.1 copy.11
  136.1 0.0 copy-done.2
  136.1 0.1 copy.12
  136.2 0.1 pad_add_fusion
  136.3 8.5 %all_to_all.15 = s32[4,16,13]{2,0,1:T(4,128)S(1)} all-to-all(s32[4,16,13]{2,0,1:T(4,128)S(1)} %pad_add_fusion), channel_id=1, replica_groups=mesh['dp'=4,'ctx'=8] {'ctx'}, dimensions={1} | all-to-all | bytes 6656 | tf_op jit(solution)/shard_map/all_to_all | solution.py:87
  144.8 0.1 reshape.15.lists_ref
  144.9 62.0 %all-gather.8.cloned.1.call-done.pairs_ref = bf16[2048,1024]{1,0:T(8,128)(2,1)} async-done(((bf16[256,1024]{1,0:T(8,128)(2,1)}), bf16[2048,1024]{1,0:T(8,128)(2,1)}) %all-gather.8.cloned.1.call-update) | async-done | bytes 4194320 | tf_op jit(solution)/shard_map/all_gather | solution.py:98
  206.9 0.0 copy-done
  206.9 40.1 %shard_map.73 = bf16[256,4096]{1,0:T(8,128)(2,1)} custom-call(s32[832]{0:T(1024)S(1)} %reshape.15.lists_ref, bf16[256,4096]{1,0:T(8,128)(2,1)S(1)} %bitcast.15, bf16[2048,1024]{1,0:T(8,128)(2,1)} %all-gather.8.cloned.1.call-done.pairs_ref), custom_call_target="tpu_custom_call" | custom-call | tf_op jit(solution)/shard_map/pallas_call | solution.py:72
  (3 shorter events, 0.0 us)
Async XLA Ops:
  6.5 61.6 %all-gather.6.cloned.1.call-start = ((), (), s32[]{:S(2)}) async-start(), calls=%async_computation.2 | async-start | bytes 10485760 | tf_op jit(solution)/shard_map/all_gather | solution.py:95
  7.3 120.8 %all-gather.4.cloned.1.call-start = ((), (), s32[]{:S(2)}) async-start(), calls=%async_computation.1 | async-start | bytes 10485760 | tf_op jit(solution)/shard_map/all_gather | solution.py:94
  8.0 198.9 %all-gather.8.cloned.1.call-start = ((), (), s32[]{:S(2)}) async-start(), calls=%async_computation.3 | async-start | bytes 4718592 | tf_op jit(solution)/shard_map/all_gather | solution.py:98
  75.2 60.8 %copy-start.1 = (s32[1,4,16,12]{2,1,3,0:T(4,128)S(1)}, s32[1,4,16,12]{2,1,3,0:T(4,128)}, u32[]{:S(2)}) copy-start(s32[1,4,16,12]{2,1,3,0:T(4,128)} %param.12) | copy-start | bytes 9220
  75.2 60.9 %copy-start.2 = (s32[1,4,16]{2,1,0:T(4,128)S(1)}, s32[1,4,16]{2,1,0:T(4,128)}, u32[]{:S(2)}) copy-start(s32[1,4,16]{2,1,0:T(4,128)} %param.13) | copy-start | bytes 772
  75.2 131.6 %copy-start = (bf16[1,256,4096]{2,1,0:T(8,128)(2,1)S(1)}, bf16[1,256,4096]{2,1,0:T(8,128)(2,1)}, u32[]{:S(2)}) copy-start(bf16[1,256,4096]{2,1,0:T(8,128)(2,1)} %param.9) | copy-start | bytes 6291460
Sparse Core Ops, SparseCore 0:
  8.9 59.2 all-gather.5
  69.7 58.2 all-gather.3
  136.1 70.7 all-gather.7

commit v2 on v1

--- a/solution.py
+++ b/solution.py
@@ -12,31 +12,40 @@
 BLK = 128
 MAXB = 12
 LOG2E = 1.4426950408889634
+PIECES = 4
+MESH = pl.DeviceIdType.MESH
 BUCKETS = (2, 4, 6, 8, 10, 12)
 
 
 def attention_kernel(heads, local_blocks, lists_ref, queries_ref, pairs_ref, out_ref):
     group = heads // KVH
-    width = MAXB + 1
+    heads_each = heads // lists_ref.shape[0]
     factor = LOG2E * HD ** (-0.5)
 
     def one(index, carry):
         block = index // heads
         head = lax.rem(index, heads)
         kv = head // group
-        base = (head * local_blocks + block) * width
-        count = lists_ref[base + MAXB]
+        source = head // heads_each
+        entry = lax.rem(head, heads_each) * local_blocks + block
+        count = lists_ref[source, entry, MAXB]
         rows = pl.ds(pl.multiple_of(block * BLK, BLK), BLK)
         columns = pl.ds(pl.multiple_of(head * HD, HD), HD)
         key_columns = pl.ds(pl.multiple_of(kv * HD, HD), HD)
-        value_columns = pl.ds(pl.multiple_of((KVH + kv) * HD, HD), HD)
 
         def attend(slots):
             query = queries_ref[rows, columns]
+            chosen = [lists_ref[source, entry, s] for s in range(slots)]
             places = [
-                pl.ds(pl.multiple_of(lists_ref[base + s] * BLK, BLK), BLK) for s in range(slots)
+                (
+                    pick // local_blocks,
+                    pl.ds(pl.multiple_of(lax.rem(pick, local_blocks) * BLK, BLK), BLK),
+                )
+                for pick in chosen
             ]
-            keys = jnp.concatenate([pairs_ref[place, key_columns] for place in places], axis=0)
+            keys = jnp.concatenate(
+                [pairs_ref[owner, 0, place, key_columns] for owner, place in places], axis=0
+            )
             scores = lax.dot_general(
                 query, keys, (((1,), (1,)), ((), ())), preferred_element_type=jnp.float32
             )
@@ -51,7 +60,9 @@
             tiles = [jnp.exp2((tile - peak) * factor) for tile in tiles]
             total = jnp.sum(functools.reduce(jnp.add, tiles), axis=1, keepdims=True)
             weights = jnp.concatenate([tile.astype(jnp.bfloat16) for tile in tiles], axis=1)
-            values = jnp.concatenate([pairs_ref[place, value_columns] for place in places], axis=0)
+            values = jnp.concatenate(
+                [pairs_ref[owner, 1, place, key_columns] for owner, place in places], axis=0
+            )
             attended = jnp.dot(weights, values, preferred_element_type=jnp.float32)
             out_ref[rows, columns] = (attended / total).astype(jnp.bfloat16)
 
@@ -82,21 +93,280 @@
     )(lists, queries, pairs)
 
 
+def gather_kernel(
+    ctx_size,
+    hidden_ref,
+    gain_ref,
+    key_ref,
+    value_ref,
+    table_ref,
+    pairs_ref,
+    tables_ref,
+    weights,
+    rows_in,
+    normed,
+    totals,
+    own_pair,
+    x_sems,
+    y_sems,
+    core_sems,
+    core_x_sems,
+    core_y_sems,
+    ring_sems,
+    table_sems,
+    local_sems,
+):
+    dp = lax.axis_index("dp")
+    ctx = lax.axis_index("ctx")
+    core = dp % 2
+    core_peer = dp + 1 - 2 * core
+    x_peer = dp + 2 - 4 * (dp // 2)
+    cross_peer = x_peer + 1 - 2 * core
+    side = ctx % 2
+    y_peer = ctx + 1 - 2 * side
+    half_ring = ctx_size // 2
+    position = (1 - side) * (ctx // 2) + side * (ctx_size - 1 - ctx // 2)
+
+    def ctx_at(place):
+        place = (place + ctx_size) % ctx_size
+        second = place // half_ring
+        return (1 - second) * 2 * place + second * (2 * (ctx_size - 1 - place) + 1)
+
+    shard = key_ref.shape[0]
+    half = shard // 2
+    chunk = half // PIECES
+    sources = (key_ref, value_ref)
+    total_pieces = 2 * PIECES
+
+    barrier = pltpu.get_barrier_semaphore()
+    for step in range(1, ctx_size):
+        pl.semaphore_signal(
+            barrier, inc=1, device_id={"ctx": (ctx + step) % ctx_size}, device_id_type=MESH
+        )
+    for peer in (core_peer, x_peer):
+        pl.semaphore_signal(barrier, inc=1, device_id={"dp": peer}, device_id_type=MESH)
+    pl.semaphore_wait(barrier, ctx_size + 1)
+
+    def remote(src, dst, sems, index, device):
+        return pltpu.make_async_remote_copy(
+            src_ref=src,
+            dst_ref=dst,
+            send_sem=sems.at[(0, *index)],
+            recv_sem=sems.at[(1, *index)],
+            device_id=device,
+            device_id_type=MESH,
+        )
+
+    def piece_rows(which, k):
+        return pl.ds(pl.multiple_of(which * half + (k % PIECES) * chunk, chunk), chunk)
+
+    x_copies, y_copies, core_copies, core_x, core_y, own_copies = [], [], [], [], [], []
+    for k in range(total_pieces):
+        j = k // PIECES
+        mine, other = piece_rows(side, k), piece_rows(1 - side, k)
+        quarter = pl.ds((k % PIECES) * 2 * chunk, 2 * chunk)
+        x_copies.append(
+            remote(sources[j].at[mine], weights.at[dp, j, mine], x_sems, (k,), {"dp": x_peer})
+        )
+        arrived = weights.at[x_peer, j, mine]
+        y_copies.append(remote(arrived, arrived, y_sems, (k,), {"ctx": y_peer}))
+        core_x.append(remote(arrived, arrived, core_x_sems, (k,), {"dp": core_peer}))
+        second = weights.at[x_peer, j, other]
+        core_y.append(remote(second, second, core_y_sems, (k,), {"dp": core_peer}))
+        core_copies.append(
+            remote(
+                sources[j].at[quarter],
+                weights.at[dp, j, quarter],
+                core_sems,
+                (k,),
+                {"dp": core_peer},
+            )
+        )
+        own_copies.append(
+            pltpu.make_async_copy(
+                sources[j].at[quarter], weights.at[dp, j, quarter], local_sems.at[k]
+            )
+        )
+
+    load = pltpu.make_async_copy(hidden_ref, rows_in, local_sems.at[total_pieces])
+    load.start()
+    for k in range(total_pieces):
+        x_copies[k].start()
+    for k in range(total_pieces):
+        core_copies[k].start()
+        own_copies[k].start()
+    own_table = pltpu.make_async_copy(
+        table_ref.at[ctx], tables_ref.at[ctx], local_sems.at[total_pieces + 1]
+    )
+    own_table.start()
+    table_copies = []
+    for step in range(1, ctx_size):
+        to = (ctx + step) % ctx_size
+        table_copies.append(
+            remote(table_ref.at[to], tables_ref.at[ctx], table_sems, (step,), {"ctx": to})
+        )
+        table_copies[-1].start()
+
+    totals[...] = jnp.zeros_like(totals)
+    load.wait()
+    strip = 16
+
+    @pl.loop(0, rows_in.shape[0] // strip)
+    def _(index):
+        rows = pl.ds(pl.multiple_of(index * strip, strip), strip)
+        upcast = rows_in[rows, :].astype(jnp.float32)
+        mean_square = jnp.mean(upcast * upcast, axis=-1, keepdims=True)
+        gain = gain_ref[...].astype(jnp.float32)
+        normed[rows, :] = (upcast * lax.rsqrt(mean_square + 1e-05) * gain).astype(jnp.bfloat16)
+
+    def accumulate(owner, j, start, size):
+        columns = pl.ds(pl.multiple_of(owner * shard + start, chunk), size)
+        totals[j] += jnp.dot(
+            normed[:, columns],
+            weights[owner, j, pl.ds(pl.multiple_of(start, chunk), size), :],
+            preferred_element_type=jnp.float32,
+        )
+
+    def ring_copy(j, way, step):
+        sign = 1 - 2 * way
+        origin = ctx_at(position - sign * step)
+        source = own_pair.at[j] if step == 0 else pairs_ref.at[origin, j]
+        return remote(
+            source,
+            pairs_ref.at[origin, j],
+            ring_sems,
+            (j, way, step),
+            {"ctx": ctx_at(position + sign)},
+        )
+
+    def hops(j, way):
+        return half_ring if j == way else half_ring - 1
+
+    sent, own_stores = [], []
+
+    def ring_start(j, step):
+        for way in range(2):
+            if step < hops(j, way):
+                copy = ring_copy(j, way, step)
+                copy.start()
+                sent.append(copy)
+
+    def ring_wait(j, step):
+        for way in range(2):
+            if step < hops(j, way):
+                ring_copy(j, way, step).wait_recv()
+
+    def finish(j):
+        own_pair[j] = totals[j].astype(jnp.bfloat16)
+        store = pltpu.make_async_copy(
+            own_pair.at[j], pairs_ref.at[ctx, j], local_sems.at[total_pieces + 2 + j]
+        )
+        store.start()
+        own_stores.append(store)
+        ring_start(j, 0)
+
+    key_step = 0
+    for k in range(total_pieces + 2):
+        if k < total_pieces:
+            x_copies[k].wait_recv()
+            y_copies[k].start()
+            core_x[k].start()
+        if 1 <= k <= total_pieces:
+            y_copies[k - 1].wait_recv()
+            core_y[k - 1].start()
+        if k < total_pieces:
+            j, at = k // PIECES, (k % PIECES) * chunk
+            own_copies[k].wait()
+            accumulate(dp, j, 2 * at, 2 * chunk)
+            core_copies[k].wait_recv()
+            accumulate(core_peer, j, 2 * at, 2 * chunk)
+            accumulate(x_peer, j, side * half + at, chunk)
+        if 1 <= k <= total_pieces:
+            j, at = (k - 1) // PIECES, ((k - 1) % PIECES) * chunk
+            accumulate(x_peer, j, (1 - side) * half + at, chunk)
+            core_x[k - 1].wait_recv()
+            accumulate(cross_peer, j, side * half + at, chunk)
+        if 2 <= k:
+            j, at = (k - 2) // PIECES, ((k - 2) % PIECES) * chunk
+            core_y[k - 2].wait_recv()
+            accumulate(cross_peer, j, (1 - side) * half + at, chunk)
+        if k == PIECES + 1:
+            finish(0)
+        if k > PIECES + 1 and key_step < half_ring - 1:
+            ring_wait(0, key_step)
+            key_step += 1
+            ring_start(0, key_step)
+    finish(1)
+    value_step = 0
+    while key_step < half_ring or value_step < half_ring:
+        for j, step in ((0, key_step), (1, value_step)):
+            if step < half_ring:
+                ring_wait(j, step)
+                if step + 1 < half_ring:
+                    ring_start(j, step + 1)
+        key_step, value_step = min(key_step + 1, half_ring), min(value_step + 1, half_ring)
+    for copy in table_copies:
+        copy.wait_recv()
+    for copy in (own_table, *own_stores):
+        copy.wait()
+    for group in (x_copies, y_copies, core_copies, core_x, core_y, sent, table_copies):
+        for copy in group:
+            copy.wait_send()
+
+
+def gather(hidden, norm_gain, key_weight, value_weight, tables, dp_size, ctx_size):
+    rows, width = hidden.shape
+    features = key_weight.shape[1]
+    pieces = 2 * PIECES
+    dma = pltpu.SemaphoreType.DMA
+    any_spec = pl.BlockSpec(memory_space=pl.ANY)
+    return pl.pallas_call(
+        functools.partial(gather_kernel, ctx_size),
+        out_shape=(
+            jax.ShapeDtypeStruct((ctx_size, 2, rows, features), jnp.bfloat16),
+            jax.ShapeDtypeStruct(tables.shape, jnp.int32),
+        ),
+        in_specs=[
+            any_spec,
+            pl.BlockSpec(memory_space=pltpu.VMEM),
+            any_spec,
+            any_spec,
+            any_spec,
+        ],
+        out_specs=(any_spec, any_spec),
+        scratch_shapes=[
+            pltpu.VMEM((dp_size, 2, width // dp_size, features), jnp.bfloat16),
+            pltpu.VMEM((rows, width), jnp.bfloat16),
+            pltpu.VMEM((rows, width), jnp.bfloat16),
+            pltpu.VMEM((2, rows, features), jnp.float32),
+            pltpu.VMEM((2, rows, features), jnp.bfloat16),
+            dma((2, pieces)),
+            dma((2, pieces)),
+            dma((2, pieces)),
+            dma((2, pieces)),
+            dma((2, pieces)),
+            dma((2, 2, 2, ctx_size // 2)),
+            dma((2, ctx_size)),
+            dma((pieces + 4,)),
+        ],
+        compiler_params=pltpu.CompilerParams(
+            collective_id=0, has_side_effects=True, vmem_limit_bytes=48 * 2**20
+        ),
+    )(hidden, norm_gain, key_weight, value_weight, tables)
+
+
 def on_device(hidden, norm_gain, queries, key_weight, value_weight, block_lists, block_counts):
+    dp_size, ctx_size = lax.axis_size("dp"), lax.axis_size("ctx")
     tables = jnp.concatenate([block_lists[0], block_counts[0][..., None]], axis=-1)
-    tables = lax.all_to_all(tables, "ctx", split_axis=1, concat_axis=0, tiled=True)
-    heads, local_blocks, _ = tables.shape
-    upcast = hidden[0].astype(jnp.float32)
-    mean_square = jnp.mean(upcast * upcast, axis=-1, keepdims=True)
-    normed = (upcast * lax.rsqrt(mean_square + 1e-05) * norm_gain.astype(jnp.float32)).astype(
-        jnp.bfloat16
+    heads_each, blocks, used = tables.shape
+    local_blocks = blocks // ctx_size
+    tables = tables.reshape(heads_each, ctx_size, local_blocks, used).swapaxes(0, 1)
+    tables = tables.reshape(ctx_size, heads_each * local_blocks, used)
+    tables = jnp.pad(tables, ((0, 0), (0, 0), (0, HD - used)))
+    pairs, lists = gather(
+        hidden[0], norm_gain[None], key_weight, value_weight, tables, dp_size, ctx_size
     )
-    key_all = lax.all_gather(key_weight, "dp", axis=0, tiled=True)
-    value_all = lax.all_gather(value_weight, "dp", axis=0, tiled=True)
-    keys = jnp.dot(normed, key_all, preferred_element_type=jnp.float32).astype(jnp.bfloat16)
-    values = jnp.dot(normed, value_all, preferred_element_type=jnp.float32).astype(jnp.bfloat16)
-    pairs = lax.all_gather(jnp.concatenate([keys, values], axis=1), "ctx", axis=0, tiled=True)
-    return attention(tables.reshape(-1), queries[0], pairs, heads, local_blocks)[None]
+    return attention(lists, queries[0], pairs, heads_each * ctx_size, local_blocks)[None]
 
 
 def solution(mesh):

time: 256 us -> 156 us (0.61)
  waiting for transfers between devices: 172 us -> 0 us
  Pallas kernels: 40.1 us -> 149 us
  matrix products: 14.1 us -> 0 us
  between operations: 13.2 us -> 0.06 us
  blocking collectives: 8.45 us -> 0 us
  local copies, waits for them, and re-layouts: 0.39 us -> 5.74 us
  other arithmetic: 4.78 us -> 0.1 us
    all_gather x3 -> x0, waiting for transfers between devices: 171 us -> none  [the longest x1 62 us: on_device(): lax.all_gather(jnp.concatenate([keys, values], axis=1), 'ctx', axis=0, ti...]
    pallas_call x0 -> x1, Pallas kernels: none -> 107 us  [gather(): pl.pallas_call(functools.partial(gather_kernel, ctx_size), out_shape=(jax...]
    dot_general x2 -> x0, matrix products: 14.1 us -> none  [the longest x1 7.04 us: on_device(): jnp.dot(normed, value_all, preferred_element_type=jnp.float32)]
    all_to_all x1 -> x0, blocking collectives: 8.45 us -> none  [on_device(): lax.all_to_all(tables, 'ctx', split_axis=1, concat_axis=0, tiled=True)]
    unnamed x7 -> x8, local copies, waits for them, and re-layouts: 0.13 us -> 4.77 us
    reduce_sum x1 -> x0, other arithmetic: 3.1 us -> none  [on_device(): mean_square = jnp.mean(upcast * upcast, axis=-1, keepdims=True)]
  transfers between devices with their start and end apart: 3 -> 0, of which waited for: 3 -> 0; matrix products, arithmetic and copies ran while one was open for 4% -> 0% of each run, Pallas kernels for 0% -> 0%
where the time goes in v2:
time: 156 us; the launch traced here: 155 us
  Pallas kernels  149 us (96%)
  local copies, waits for them, and re-layouts  5.74 us (4%)
    pallas_call x1, Pallas kernels, gather(): pl.pallas_call(functools.partial(gather_kernel, ctx_size), out_shape=(jax...  107 us
    pallas_call x1, Pallas kernels, attention(): pl.pallas_call(functools.partial(attention_kernel, heads, local_blocks),...  41.8 us
    unnamed x8, local copies, waits for them, and re-layouts  4.77 us

profile of v2, /device:TPU:28, one launch (start us, length us, event | category | flops | bytes accessed | tf_op | source)
XLA Modules:
  0.0 155.0 jit_solution(5012421492074909118)
XLA Ops:
  0.0 0.8 copy.12
  0.8 0.2 copy.13
  1.0 0.7 broadcast_in_dim.6.gain_ref
  1.7 0.8 copy.11
  2.5 0.1 add_bitcast_fusion
  2.7 0.0 copy-start
  2.7 1.6 %copy-done = bf16[2048,512]{1,0:T(8,128)(2,1)S(1)} copy-done((bf16[2048,512]{1,0:T(8,128)(2,1)S(1)}, bf16[2048,512]{1,0:T(8,128)(2,1)}, u32[]{:S(2)}) %copy-start) | copy-done | bytes 2097176
  4.3 0.0 copy-start.1
  4.3 1.6 %copy-done.1 = bf16[2048,512]{1,0:T(8,128)(2,1)S(1)} copy-done((bf16[2048,512]{1,0:T(8,128)(2,1)S(1)}, bf16[2048,512]{1,0:T(8,128)(2,1)}, u32[]{:S(2)}) %copy-start.1) | copy-done | bytes 2097176
  5.9 0.0 copy-start.2
  5.9 107.3 %shard_map.73 = (bf16[8,2,256,512]{3,2,1,0:T(8,128)(2,1)}, s32[8,8,128]{2,1,0:T(8,128)S(1)}) custom-call(bf16[256,8192]{1,0:T(8,128)(2,1)} %bitcast.9, bf16[1,8192]{1,0:T(2,128)(2,1)S(1)} %broadcast_in_dim.6.gain_ref, bf16[2048,512]{1,0:T(8,128)(2,1)S(1)} %copy-done, bf16[2048,512]{1,0:T(8,128)(2,1)S(1)} %copy-done.1, s32[8,8,128]{2,1,0:T(8,128)S(1)} %pad.4.table_ref), custom_call_target="tpu_custom_call" | custom-call | tf_op jit(solution)/shard_map/pallas_call | solution.py:323
  113.2 0.0 copy-done.2
  113.2 41.8 %shard_map.74 = bf16[256,4096]{1,0:T(8,128)(2,1)} custom-call(s32[8,8,128]{2,1,0:T(8,128)S(1)} %get-tuple-element.7.lists_ref, bf16[256,4096]{1,0:T(8,128)(2,1)S(1)} %bitcast.8, bf16[8,2,256,512]{3,2,1,0:T(8,128)(2,1)} %get-tuple-element.8.pairs_ref), custom_call_target="tpu_custom_call" | custom-call | tf_op jit(solution)/shard_map/pallas_call | solution.py:83
  (2 shorter events, 0.0 us)
Async XLA Ops:
  2.7 1.6 %copy-start = (bf16[2048,512]{1,0:T(8,128)(2,1)S(1)}, bf16[2048,512]{1,0:T(8,128)(2,1)}, u32[]{:S(2)}) copy-start(bf16[2048,512]{1,0:T(8,128)(2,1)} %key_ref.1) | copy-start | bytes 6291460
  4.3 1.6 %copy-start.1 = (bf16[2048,512]{1,0:T(8,128)(2,1)S(1)}, bf16[2048,512]{1,0:T(8,128)(2,1)}, u32[]{:S(2)}) copy-start(bf16[2048,512]{1,0:T(8,128)(2,1)} %value_ref.1) | copy-start | bytes 6291460
  5.9 107.3 %copy-start.2 = (bf16[1,256,4096]{2,1,0:T(8,128)(2,1)S(1)}, bf16[1,256,4096]{2,1,0:T(8,128)(2,1)}, u32[]{:S(2)}) copy-start(bf16[1,256,4096]{2,1,0:T(8,128)(2,1)} %param.9) | copy-start | bytes 6291460

commit v3 on v2

--- a/solution.py
+++ b/solution.py
@@ -12,7 +12,9 @@
 BLK = 128
 MAXB = 12
 LOG2E = 1.4426950408889634
-PIECES = 4
+CHUNKS = 8
+DIRECT = 5
+RELAYED = CHUNKS - DIRECT
 MESH = pl.DeviceIdType.MESH
 BUCKETS = (2, 4, 6, 8, 10, 12)
 
@@ -22,61 +24,75 @@
     heads_each = heads // lists_ref.shape[0]
     factor = LOG2E * HD ** (-0.5)
 
-    def one(index, carry):
-        block = index // heads
-        head = lax.rem(index, heads)
-        kv = head // group
+    def one(head, carry):
+        key_columns = pl.ds(pl.multiple_of(head // group * HD, HD), HD)
+        columns = pl.ds(pl.multiple_of(head * HD, HD), HD)
         source = head // heads_each
-        entry = lax.rem(head, heads_each) * local_blocks + block
-        count = lists_ref[source, entry, MAXB]
-        rows = pl.ds(pl.multiple_of(block * BLK, BLK), BLK)
-        columns = pl.ds(pl.multiple_of(head * HD, HD), HD)
-        key_columns = pl.ds(pl.multiple_of(kv * HD, HD), HD)
+        first = lax.rem(head, heads_each) * local_blocks
+        counts = [lists_ref[source, first + block, MAXB] for block in range(local_blocks)]
+        most = functools.reduce(jnp.maximum, counts)
+
+        def gathered(which, places):
+            return jnp.concatenate(
+                [pairs_ref[owner, which, place, key_columns] for owner, place in places], axis=0
+            )
 
         def attend(slots):
-            query = queries_ref[rows, columns]
-            chosen = [lists_ref[source, entry, s] for s in range(slots)]
-            places = [
-                (
-                    pick // local_blocks,
-                    pl.ds(pl.multiple_of(lax.rem(pick, local_blocks) * BLK, BLK), BLK),
-                )
-                for pick in chosen
-            ]
-            keys = jnp.concatenate(
-                [pairs_ref[owner, 0, place, key_columns] for owner, place in places], axis=0
-            )
-            scores = lax.dot_general(
-                query, keys, (((1,), (1,)), ((), ())), preferred_element_type=jnp.float32
-            )
-            tiles = [scores[:, s * BLK : (s + 1) * BLK] for s in range(slots)]
             row = lax.broadcasted_iota(jnp.int32, (BLK, BLK), 0)
             column = lax.broadcasted_iota(jnp.int32, (BLK, BLK), 1)
-            tiles[0] = jnp.where(column <= row, tiles[0], -jnp.inf)
-            for s in range(max(1, slots - 1), slots):
-                tiles[s] = jnp.where(s < count, tiles[s], -jnp.inf)
-            peak = functools.reduce(jnp.maximum, tiles)
-            peak = jnp.max(peak, axis=1, keepdims=True)
-            tiles = [jnp.exp2((tile - peak) * factor) for tile in tiles]
-            total = jnp.sum(functools.reduce(jnp.add, tiles), axis=1, keepdims=True)
-            weights = jnp.concatenate([tile.astype(jnp.bfloat16) for tile in tiles], axis=1)
-            values = jnp.concatenate(
-                [pairs_ref[owner, 1, place, key_columns] for owner, place in places], axis=0
-            )
-            attended = jnp.dot(weights, values, preferred_element_type=jnp.float32)
-            out_ref[rows, columns] = (attended / total).astype(jnp.bfloat16)
+            places, scores, weights, totals = [], [], [], []
+            for block in range(local_blocks):
+                chosen = [lists_ref[source, first + block, s] for s in range(slots)]
+                places.append(
+                    [
+                        (
+                            pick // local_blocks,
+                            pl.ds(pl.multiple_of(lax.rem(pick, local_blocks) * BLK, BLK), BLK),
+                        )
+                        for pick in chosen
+                    ]
+                )
+                scores.append(
+                    lax.dot_general(
+                        queries_ref[block * BLK : (block + 1) * BLK, columns],
+                        gathered(0, places[block]),
+                        (((1,), (1,)), ((), ())),
+                        preferred_element_type=jnp.float32,
+                    )
+                )
+            for block in range(local_blocks):
+                tiles = [scores[block][:, s * BLK : (s + 1) * BLK] for s in range(slots)]
+                tiles[0] = jnp.where(column <= row, tiles[0], -jnp.inf)
+                for s in range(1, slots):
+                    tiles[s] = jnp.where(s < counts[block], tiles[s], -jnp.inf)
+                peak = functools.reduce(jnp.maximum, tiles)
+                peak = jnp.max(peak, axis=1, keepdims=True)
+                tiles = [jnp.exp2((tile - peak) * factor) for tile in tiles]
+                totals.append(jnp.sum(functools.reduce(jnp.add, tiles), axis=1, keepdims=True))
+                weights.append(
+                    jnp.concatenate([tile.astype(jnp.bfloat16) for tile in tiles], axis=1)
+                )
+            for block in range(local_blocks):
+                attended = jnp.dot(
+                    weights[block],
+                    gathered(1, places[block]),
+                    preferred_element_type=jnp.float32,
+                )
+                out_ref[block * BLK : (block + 1) * BLK, columns] = (
+                    attended / totals[block]
+                ).astype(jnp.bfloat16)
 
         below = 0
         for slots in BUCKETS:
 
-            @pl.when((count > below) & (count <= slots))
+            @pl.when((most > below) & (most <= slots))
             def _(slots=slots):
                 attend(slots)
 
             below = slots
         return carry
 
-    lax.fori_loop(0, heads * local_blocks, one, 0)
+    lax.fori_loop(0, heads, one, 0)
 
 
 def attention(lists, queries, pairs, heads, local_blocks):
@@ -133,10 +149,9 @@
         return (1 - second) * 2 * place + second * (2 * (ctx_size - 1 - place) + 1)
 
     shard = key_ref.shape[0]
-    half = shard // 2
-    chunk = half // PIECES
+    chunk = shard // CHUNKS
     sources = (key_ref, value_ref)
-    total_pieces = 2 * PIECES
+    total_pieces = 2 * DIRECT
 
     barrier = pltpu.get_barrier_semaphore()
     for step in range(1, ctx_size):
@@ -157,22 +172,20 @@
             device_id_type=MESH,
         )
 
-    def piece_rows(which, k):
-        return pl.ds(pl.multiple_of(which * half + (k % PIECES) * chunk, chunk), chunk)
-
-    x_copies, y_copies, core_copies, core_x, core_y, own_copies = [], [], [], [], [], []
-    for k in range(total_pieces):
-        j = k // PIECES
-        mine, other = piece_rows(side, k), piece_rows(1 - side, k)
-        quarter = pl.ds((k % PIECES) * 2 * chunk, 2 * chunk)
-        x_copies.append(
-            remote(sources[j].at[mine], weights.at[dp, j, mine], x_sems, (k,), {"dp": x_peer})
-        )
-        arrived = weights.at[x_peer, j, mine]
-        y_copies.append(remote(arrived, arrived, y_sems, (k,), {"ctx": y_peer}))
-        core_x.append(remote(arrived, arrived, core_x_sems, (k,), {"dp": core_peer}))
-        second = weights.at[x_peer, j, other]
-        core_y.append(remote(second, second, core_y_sems, (k,), {"dp": core_peer}))
+    def start_of(which, m):
+        return (m + which * (CHUNKS - 1 - 2 * m)) * chunk
+
+    def rows_of(which, m):
+        return pl.ds(pl.multiple_of(start_of(which, m), chunk), chunk)
+
+    def is_relayed(k):
+        return k % DIRECT < RELAYED
+
+    quarter_size = shard // 4
+    x_copies, y_copies, core_copies, core_x, core_y, own_copies = [], {}, [], [], {}, []
+    for k in range(8):
+        j = k // 4
+        quarter = pl.ds((k % 4) * quarter_size, quarter_size)
         core_copies.append(
             remote(
                 sources[j].at[quarter],
@@ -187,16 +200,28 @@
                 sources[j].at[quarter], weights.at[dp, j, quarter], local_sems.at[k]
             )
         )
-
-    load = pltpu.make_async_copy(hidden_ref, rows_in, local_sems.at[total_pieces])
+    for k in range(total_pieces):
+        j = k // DIRECT
+        mine, other = rows_of(side, k % DIRECT), rows_of(1 - side, k % DIRECT)
+        x_copies.append(
+            remote(sources[j].at[mine], weights.at[dp, j, mine], x_sems, (k,), {"dp": x_peer})
+        )
+        arrived = weights.at[x_peer, j, mine]
+        core_x.append(remote(arrived, arrived, core_x_sems, (k,), {"dp": core_peer}))
+        if is_relayed(k):
+            y_copies[k] = remote(arrived, arrived, y_sems, (k,), {"ctx": y_peer})
+            second = weights.at[x_peer, j, other]
+            core_y[k] = remote(second, second, core_y_sems, (k,), {"dp": core_peer})
+
+    load = pltpu.make_async_copy(hidden_ref, rows_in, local_sems.at[8])
     load.start()
     for k in range(total_pieces):
         x_copies[k].start()
-    for k in range(total_pieces):
+    for k in range(8):
         core_copies[k].start()
         own_copies[k].start()
     own_table = pltpu.make_async_copy(
-        table_ref.at[ctx], tables_ref.at[ctx], local_sems.at[total_pieces + 1]
+        table_ref.at[ctx], tables_ref.at[ctx], local_sems.at[8 + 1]
     )
     own_table.start()
     table_copies = []
@@ -259,40 +284,44 @@
     def finish(j):
         own_pair[j] = totals[j].astype(jnp.bfloat16)
         store = pltpu.make_async_copy(
-            own_pair.at[j], pairs_ref.at[ctx, j], local_sems.at[total_pieces + 2 + j]
+            own_pair.at[j], pairs_ref.at[ctx, j], local_sems.at[8 + 2 + j]
         )
         store.start()
         own_stores.append(store)
         ring_start(j, 0)
 
     key_step = 0
-    for k in range(total_pieces + 2):
+    for k in range(total_pieces + 1):
         if k < total_pieces:
             x_copies[k].wait_recv()
-            y_copies[k].start()
+            if is_relayed(k):
+                y_copies[k].start()
             core_x[k].start()
-        if 1 <= k <= total_pieces:
+        if k - 1 in y_copies:
             y_copies[k - 1].wait_recv()
             core_y[k - 1].start()
         if k < total_pieces:
-            j, at = k // PIECES, (k % PIECES) * chunk
-            own_copies[k].wait()
-            accumulate(dp, j, 2 * at, 2 * chunk)
-            core_copies[k].wait_recv()
-            accumulate(core_peer, j, 2 * at, 2 * chunk)
-            accumulate(x_peer, j, side * half + at, chunk)
+            j, m = k // DIRECT, k % DIRECT
+            if m < 4:
+                quarter = 4 * j + m
+                own_copies[quarter].wait()
+                accumulate(dp, j, m * quarter_size, quarter_size)
+                core_copies[quarter].wait_recv()
+                accumulate(core_peer, j, m * quarter_size, quarter_size)
+            accumulate(x_peer, j, start_of(side, m), chunk)
         if 1 <= k <= total_pieces:
-            j, at = (k - 1) // PIECES, ((k - 1) % PIECES) * chunk
-            accumulate(x_peer, j, (1 - side) * half + at, chunk)
+            j, m = (k - 1) // DIRECT, (k - 1) % DIRECT
+            if is_relayed(k - 1):
+                accumulate(x_peer, j, start_of(1 - side, m), chunk)
             core_x[k - 1].wait_recv()
-            accumulate(cross_peer, j, side * half + at, chunk)
-        if 2 <= k:
-            j, at = (k - 2) // PIECES, ((k - 2) % PIECES) * chunk
+            accumulate(cross_peer, j, start_of(side, m), chunk)
+        if k - 2 in core_y:
+            j, m = (k - 2) // DIRECT, (k - 2) % DIRECT
             core_y[k - 2].wait_recv()
-            accumulate(cross_peer, j, (1 - side) * half + at, chunk)
-        if k == PIECES + 1:
+            accumulate(cross_peer, j, start_of(1 - side, m), chunk)
+        if k == DIRECT:
             finish(0)
-        if k > PIECES + 1 and key_step < half_ring - 1:
+        if k > DIRECT and key_step < half_ring - 1:
             ring_wait(0, key_step)
             key_step += 1
             ring_start(0, key_step)
@@ -309,7 +338,15 @@
         copy.wait_recv()
     for copy in (own_table, *own_stores):
         copy.wait()
-    for group in (x_copies, y_copies, core_copies, core_x, core_y, sent, table_copies):
+    for group in (
+        x_copies,
+        y_copies.values(),
+        core_copies,
+        core_x,
+        core_y.values(),
+        sent,
+        table_copies,
+    ):
         for copy in group:
             copy.wait_send()
 
@@ -317,7 +354,7 @@
 def gather(hidden, norm_gain, key_weight, value_weight, tables, dp_size, ctx_size):
     rows, width = hidden.shape
     features = key_weight.shape[1]
-    pieces = 2 * PIECES
+    pieces = 2 * DIRECT
     dma = pltpu.SemaphoreType.DMA
     any_spec = pl.BlockSpec(memory_space=pl.ANY)
     return pl.pallas_call(
@@ -342,15 +379,15 @@
             pltpu.VMEM((2, rows, features), jnp.bfloat16),
             dma((2, pieces)),
             dma((2, pieces)),
-            dma((2, pieces)),
+            dma((2, 8)),
             dma((2, pieces)),
             dma((2, pieces)),
             dma((2, 2, 2, ctx_size // 2)),
             dma((2, ctx_size)),
-            dma((pieces + 4,)),
+            dma((12,)),
         ],
         compiler_params=pltpu.CompilerParams(
-            collective_id=0, has_side_effects=True, vmem_limit_bytes=48 * 2**20
+            collective_id=0, has_side_effects=True, vmem_limit_bytes=62 * 2**20
         ),
     )(hidden, norm_gain, key_weight, value_weight, tables)
 

time: 156 us -> 139 us (0.89)
  Pallas kernels: 149 us -> 133 us
    pallas_call x1, Pallas kernels: 41.8 us -> 26.9 us  [attention(): pl.pallas_call(functools.partial(attention_kernel, heads, local_blocks),...]
    unnamed x8 -> x6, local copies, waits for them, and re-layouts: 4.77 us -> 3.93 us
where the time goes in v3:
time: 139 us
  Pallas kernels  133 us (96%)
  local copies, waits for them, and re-layouts  6.12 us (4%)
    pallas_call x1, Pallas kernels, gather(): pl.pallas_call(functools.partial(gather_kernel, ctx_size), out_shape=(jax...  106 us
    pallas_call x1, Pallas kernels, attention(): pl.pallas_call(functools.partial(attention_kernel, heads, local_blocks),...  26.9 us
    unnamed x6, local copies, waits for them, and re-layouts  3.93 us

profile of v3, /device:TPU:28, one launch (start us, length us, event | category | flops | bytes accessed | tf_op | source)
XLA Modules:
  0.0 138.9 jit_solution(189384550325329223)
XLA Ops:
  0.0 0.8 copy.12
  0.8 0.2 copy.13
  1.0 1.4 broadcast_in_dim.6.gain_ref
  2.3 0.8 copy.11
  3.2 0.1 add_bitcast_fusion
  3.3 0.6 pad.4.table_ref
  3.9 105.7 %shard_map.73 = (bf16[8,2,256,512]{3,2,1,0:T(8,128)(2,1)}, s32[8,8,128]{2,1,0:T(8,128)}) custom-call(bf16[256,8192]{1,0:T(8,128)(2,1)} %bitcast.9, bf16[1,8192]{1,0:T(2,128)(2,1)} %broadcast_in_dim.6.gain_ref, bf16[2048,512]{1,0:T(8,128)(2,1)} %key_ref.1, bf16[2048,512]{1,0:T(8,128)(2,1)} %value_ref.1, s32[8,8,128]{2,1,0:T(8,128)} %pad.4.table_ref), custom_call_target="tpu_custom_call" | custom-call | tf_op jit(solution)/shard_map/pallas_call | solution.py:360
  109.7 0.0 copy-start
  109.7 1.6 %copy-done = bf16[1,256,4096]{2,1,0:T(8,128)(2,1)S(1)} copy-done((bf16[1,256,4096]{2,1,0:T(8,128)(2,1)S(1)}, bf16[1,256,4096]{2,1,0:T(8,128)(2,1)}, u32[]{:S(2)}) %copy-start) | copy-done | bytes 2097176
  111.2 0.0 copy-start.1
  111.2 0.8 copy-done.1
  112.0 26.9 %shard_map.74 = bf16[256,4096]{1,0:T(8,128)(2,1)} custom-call(s32[8,8,128]{2,1,0:T(8,128)S(1)} %copy-done.1, bf16[256,4096]{1,0:T(8,128)(2,1)S(1)} %bitcast.8, bf16[8,2,256,512]{3,2,1,0:T(8,128)(2,1)} %get-tuple-element.8.pairs_ref), custom_call_target="tpu_custom_call" | custom-call | tf_op jit(solution)/shard_map/pallas_call | solution.py:99
  (1 shorter events, 0.0 us)
Async XLA Ops:
  109.7 1.6 %copy-start = (bf16[1,256,4096]{2,1,0:T(8,128)(2,1)S(1)}, bf16[1,256,4096]{2,1,0:T(8,128)(2,1)}, u32[]{:S(2)}) copy-start(bf16[1,256,4096]{2,1,0:T(8,128)(2,1)} %param.9) | copy-start | bytes 6291460
  111.2 0.8 copy-start.1

commit v4 on v3

--- a/solution.py
+++ b/solution.py
@@ -12,6 +12,7 @@
 BLK = 128
 MAXB = 12
 LOG2E = 1.4426950408889634
+PARTS = 4
 CHUNKS = 8
 DIRECT = 5
 RELAYED = CHUNKS - DIRECT
@@ -19,22 +20,23 @@
 BUCKETS = (2, 4, 6, 8, 10, 12)
 
 
-def attention_kernel(heads, local_blocks, lists_ref, queries_ref, pairs_ref, out_ref):
+def attention_kernel(heads, local_blocks, lists_ref, queries_ref, keys_ref, values_ref, out_ref):
     group = heads // KVH
+    first_head = pl.program_id(0) * group
     heads_each = heads // lists_ref.shape[0]
     factor = LOG2E * HD ** (-0.5)
 
-    def one(head, carry):
-        key_columns = pl.ds(pl.multiple_of(head // group * HD, HD), HD)
-        columns = pl.ds(pl.multiple_of(head * HD, HD), HD)
+    def one(step, carry):
+        head = first_head + step
+        columns = pl.ds(pl.multiple_of(step * HD, HD), HD)
         source = head // heads_each
         first = lax.rem(head, heads_each) * local_blocks
         counts = [lists_ref[source, first + block, MAXB] for block in range(local_blocks)]
         most = functools.reduce(jnp.maximum, counts)
 
-        def gathered(which, places):
+        def gathered(ref, places):
             return jnp.concatenate(
-                [pairs_ref[owner, which, place, key_columns] for owner, place in places], axis=0
+                [ref[owner, 0, place, :] for owner, place in places], axis=0
             )
 
         def attend(slots):
@@ -55,7 +57,7 @@
                 scores.append(
                     lax.dot_general(
                         queries_ref[block * BLK : (block + 1) * BLK, columns],
-                        gathered(0, places[block]),
+                        gathered(keys_ref, places[block]),
                         (((1,), (1,)), ((), ())),
                         preferred_element_type=jnp.float32,
                     )
@@ -75,7 +77,7 @@
             for block in range(local_blocks):
                 attended = jnp.dot(
                     weights[block],
-                    gathered(1, places[block]),
+                    gathered(values_ref, places[block]),
                     preferred_element_type=jnp.float32,
                 )
                 out_ref[block * BLK : (block + 1) * BLK, columns] = (
@@ -92,21 +94,28 @@
             below = slots
         return carry
 
-    lax.fori_loop(0, heads, one, 0)
+    lax.fori_loop(0, group, one, 0)
 
 
 def attention(lists, queries, pairs, heads, local_blocks):
+    rows, width = queries.shape
+    per_part = PARTS // 2
+    shared = KVH // per_part
+    wide = pl.BlockSpec((rows, width // KVH), lambda g: (0, g))
+    block = (pairs.shape[0], 1, rows, HD)
     return pl.pallas_call(
         functools.partial(attention_kernel, heads, local_blocks),
+        grid=(KVH,),
         out_shape=jax.ShapeDtypeStruct(queries.shape, jnp.bfloat16),
         in_specs=[
             pl.BlockSpec(memory_space=pltpu.SMEM),
-            pl.BlockSpec(memory_space=pltpu.VMEM),
-            pl.BlockSpec(memory_space=pltpu.VMEM),
+            wide,
+            pl.BlockSpec(block, lambda g: (0, g // shared, 0, g % shared)),
+            pl.BlockSpec(block, lambda g: (0, per_part + g // shared, 0, g % shared)),
         ],
-        out_specs=pl.BlockSpec(memory_space=pltpu.VMEM),
-        compiler_params=pltpu.CompilerParams(vmem_limit_bytes=48 * 2**20),
-    )(lists, queries, pairs)
+        out_specs=wide,
+        compiler_params=pltpu.CompilerParams(vmem_limit_bytes=62 * 2**20),
+    )(lists, queries, pairs, pairs)
 
 
 def gather_kernel(
@@ -150,8 +159,13 @@
 
     shard = key_ref.shape[0]
     chunk = shard // CHUNKS
-    sources = (key_ref, value_ref)
-    total_pieces = 2 * DIRECT
+    features = key_ref.shape[1] * 2 // PARTS
+    total_pieces = PARTS * DIRECT
+
+    def source(j, rows):
+        ref = (key_ref, value_ref)[j * 2 // PARTS]
+        return ref.at[rows, pl.ds(j % (PARTS // 2) * features, features)]
+
 
     barrier = pltpu.get_barrier_semaphore()
     for step in range(1, ctx_size):
@@ -183,12 +197,12 @@
 
     quarter_size = shard // 4
     x_copies, y_copies, core_copies, core_x, core_y, own_copies = [], {}, [], [], {}, []
-    for k in range(8):
+    for k in range(4 * PARTS):
         j = k // 4
         quarter = pl.ds((k % 4) * quarter_size, quarter_size)
         core_copies.append(
             remote(
-                sources[j].at[quarter],
+                source(j, quarter),
                 weights.at[dp, j, quarter],
                 core_sems,
                 (k,),
@@ -197,14 +211,14 @@
         )
         own_copies.append(
             pltpu.make_async_copy(
-                sources[j].at[quarter], weights.at[dp, j, quarter], local_sems.at[k]
+                source(j, quarter), weights.at[dp, j, quarter], local_sems.at[k]
             )
         )
     for k in range(total_pieces):
         j = k // DIRECT
         mine, other = rows_of(side, k % DIRECT), rows_of(1 - side, k % DIRECT)
         x_copies.append(
-            remote(sources[j].at[mine], weights.at[dp, j, mine], x_sems, (k,), {"dp": x_peer})
+            remote(source(j, mine), weights.at[dp, j, mine], x_sems, (k,), {"dp": x_peer})
         )
         arrived = weights.at[x_peer, j, mine]
         core_x.append(remote(arrived, arrived, core_x_sems, (k,), {"dp": core_peer}))
@@ -213,15 +227,15 @@
             second = weights.at[x_peer, j, other]
             core_y[k] = remote(second, second, core_y_sems, (k,), {"dp": core_peer})
 
-    load = pltpu.make_async_copy(hidden_ref, rows_in, local_sems.at[8])
+    load = pltpu.make_async_copy(hidden_ref, rows_in, local_sems.at[4 * PARTS])
     load.start()
     for k in range(total_pieces):
         x_copies[k].start()
-    for k in range(8):
+    for k in range(4 * PARTS):
         core_copies[k].start()
         own_copies[k].start()
     own_table = pltpu.make_async_copy(
-        table_ref.at[ctx], tables_ref.at[ctx], local_sems.at[8 + 1]
+        table_ref.at[ctx], tables_ref.at[ctx], local_sems.at[4 * PARTS + 1]
     )
     own_table.start()
     table_copies = []
@@ -265,7 +279,7 @@
         )
 
     def hops(j, way):
-        return half_ring if j == way else half_ring - 1
+        return half_ring if j % 2 == way else half_ring - 1
 
     sent, own_stores = [], []
 
@@ -284,13 +298,23 @@
     def finish(j):
         own_pair[j] = totals[j].astype(jnp.bfloat16)
         store = pltpu.make_async_copy(
-            own_pair.at[j], pairs_ref.at[ctx, j], local_sems.at[8 + 2 + j]
+            own_pair.at[j], pairs_ref.at[ctx, j], local_sems.at[4 * PARTS + 2 + j]
         )
         store.start()
         own_stores.append(store)
         ring_start(j, 0)
 
-    key_step = 0
+    steps = {}
+
+    def advance():
+        for j in list(steps):
+            ring_wait(j, steps[j])
+            steps[j] += 1
+            if steps[j] == half_ring:
+                del steps[j]
+            else:
+                ring_start(j, steps[j])
+
     for k in range(total_pieces + 1):
         if k < total_pieces:
             x_copies[k].wait_recv()
@@ -319,21 +343,13 @@
             j, m = (k - 2) // DIRECT, (k - 2) % DIRECT
             core_y[k - 2].wait_recv()
             accumulate(cross_peer, j, start_of(1 - side, m), chunk)
-        if k == DIRECT:
-            finish(0)
-        if k > DIRECT and key_step < half_ring - 1:
-            ring_wait(0, key_step)
-            key_step += 1
-            ring_start(0, key_step)
-    finish(1)
-    value_step = 0
-    while key_step < half_ring or value_step < half_ring:
-        for j, step in ((0, key_step), (1, value_step)):
-            if step < half_ring:
-                ring_wait(j, step)
-                if step + 1 < half_ring:
-                    ring_start(j, step + 1)
-        key_step, value_step = min(key_step + 1, half_ring), min(value_step + 1, half_ring)
+        if k > DIRECT:
+            advance()
+        if k and k % DIRECT == 0:
+            finish(k // DIRECT - 1)
+            steps[k // DIRECT - 1] = 0
+    while steps:
+        advance()
     for copy in table_copies:
         copy.wait_recv()
     for copy in (own_table, *own_stores):
@@ -353,14 +369,14 @@
 
 def gather(hidden, norm_gain, key_weight, value_weight, tables, dp_size, ctx_size):
     rows, width = hidden.shape
-    features = key_weight.shape[1]
-    pieces = 2 * DIRECT
+    features = key_weight.shape[1] * 2 // PARTS
+    pieces = PARTS * DIRECT
     dma = pltpu.SemaphoreType.DMA
     any_spec = pl.BlockSpec(memory_space=pl.ANY)
     return pl.pallas_call(
         functools.partial(gather_kernel, ctx_size),
         out_shape=(
-            jax.ShapeDtypeStruct((ctx_size, 2, rows, features), jnp.bfloat16),
+            jax.ShapeDtypeStruct((ctx_size, PARTS, rows, features), jnp.bfloat16),
             jax.ShapeDtypeStruct(tables.shape, jnp.int32),
         ),
         in_specs=[
@@ -372,19 +388,19 @@
         ],
         out_specs=(any_spec, any_spec),
         scratch_shapes=[
-            pltpu.VMEM((dp_size, 2, width // dp_size, features), jnp.bfloat16),
+            pltpu.VMEM((dp_size, PARTS, width // dp_size, features), jnp.bfloat16),
             pltpu.VMEM((rows, width), jnp.bfloat16),
             pltpu.VMEM((rows, width), jnp.bfloat16),
-            pltpu.VMEM((2, rows, features), jnp.float32),
-            pltpu.VMEM((2, rows, features), jnp.bfloat16),
+            pltpu.VMEM((PARTS, rows, features), jnp.float32),
+            pltpu.VMEM((PARTS, rows, features), jnp.bfloat16),
             dma((2, pieces)),
             dma((2, pieces)),
-            dma((2, 8)),
+            dma((2, 4 * PARTS)),
             dma((2, pieces)),
             dma((2, pieces)),
-            dma((2, 2, 2, ctx_size // 2)),
+            dma((2, PARTS, 2, ctx_size // 2)),
             dma((2, ctx_size)),
-            dma((12,)),
+            dma((5 * PARTS + 2,)),
         ],
         compiler_params=pltpu.CompilerParams(
             collective_id=0, has_side_effects=True, vmem_limit_bytes=62 * 2**20

time: 139 us -> 142 us (1.022)
  Pallas kernels: 133 us -> 138 us
  local copies, waits for them, and re-layouts: 6.12 us -> 3.8 us
    pallas_call x1, Pallas kernels: 106 us -> 113 us  [gather(): pl.pallas_call(functools.partial(gather_kernel, ctx_size), out_shape=(jax...]
    unnamed x6 -> x2, local copies, waits for them, and re-layouts: 3.93 us -> 1.59 us
where the time goes in v4:
time: 142 us
  Pallas kernels  138 us (97%)
  local copies, waits for them, and re-layouts  3.8 us (3%)
    pallas_call x1, Pallas kernels, gather(): pl.pallas_call(functools.partial(gather_kernel, ctx_size), out_shape=(jax...  113 us
    pallas_call x1, Pallas kernels, attention(): pl.pallas_call(functools.partial(attention_kernel, heads, local_blocks),...  25.7 us

profile of v4, /device:TPU:28, one launch (start us, length us, event | category | flops | bytes accessed | tf_op | source)
XLA Modules:
  0.0 142.2 jit_solution(16975013587390838542)
XLA Ops:
  0.0 0.8 copy.12
  0.8 0.2 copy.13
  1.0 1.4 broadcast_in_dim.6.gain_ref
  2.3 0.8 copy.11
  3.2 0.1 add_bitcast_fusion
  3.3 0.6 pad.4.table_ref
  3.9 112.5 %shard_map.73 = (bf16[8,4,256,256]{3,2,1,0:T(8,128)(2,1)}, s32[8,8,128]{2,1,0:T(8,128)}) custom-call(bf16[256,8192]{1,0:T(8,128)(2,1)} %bitcast.8, bf16[1,8192]{1,0:T(2,128)(2,1)} %broadcast_in_dim.6.gain_ref, bf16[2048,512]{1,0:T(8,128)(2,1)} %key_ref.1, bf16[2048,512]{1,0:T(8,128)(2,1)} %value_ref.1, s32[8,8,128]{2,1,0:T(8,128)} %pad.4.table_ref), custom_call_target="tpu_custom_call" | custom-call | tf_op jit(solution)/shard_map/pallas_call | solution.py:376
  116.5 25.7 %shard_map.74 = bf16[256,4096]{1,0:T(8,128)(2,1)} custom-call(s32[8,8,128]{2,1,0:T(8,128)} %get-tuple-element.7.lists_ref, bf16[256,4096]{1,0:T(8,128)(2,1)} %bitcast.9, bf16[8,4,256,256]{3,2,1,0:T(8,128)(2,1)} %get-tuple-element.8.keys_ref.values_ref, bf16[8,4,256,256]{3,2,1,0:T(8,128)(2,1)} %get-tuple-element.8.keys_ref.values_ref), custom_call_target="tpu_custom_call" | custom-call | tf_op jit(solution)/shard_map/pallas_call | solution.py:106
  (1 shorter events, 0.0 us)

commit v5 on v4

--- a/solution.py
+++ b/solution.py
@@ -12,7 +12,7 @@
 BLK = 128
 MAXB = 12
 LOG2E = 1.4426950408889634
-PARTS = 4
+PARTS = 2
 CHUNKS = 8
 DIRECT = 5
 RELAYED = CHUNKS - DIRECT

time: 142 us -> 142 us (level)
  no operation moved by 1% of the time
where the time goes in v5:
time: 142 us
  Pallas kernels  138 us (97%)
  local copies, waits for them, and re-layouts  3.8 us (3%)
    pallas_call x1, Pallas kernels, gather(): pl.pallas_call(functools.partial(gather_kernel, ctx_size), out_shape=(jax...  113 us
    pallas_call x1, Pallas kernels, attention(): pl.pallas_call(functools.partial(attention_kernel, heads, local_blocks),...  25.6 us

profile of v5, /device:TPU:28, one launch (start us, length us, event | category | flops | bytes accessed | tf_op | source)
XLA Modules:
  0.0 142.1 jit_solution(8537979445357537150)
XLA Ops:
  0.0 0.8 copy.12
  0.8 0.2 copy.13
  1.0 1.4 broadcast_in_dim.6.gain_ref
  2.3 0.8 copy.11
  3.2 0.1 add_bitcast_fusion
  3.3 0.6 pad.4.table_ref
  3.9 112.5 %shard_map.73 = (bf16[8,2,256,512]{3,2,1,0:T(8,128)(2,1)}, s32[8,8,128]{2,1,0:T(8,128)}) custom-call(bf16[256,8192]{1,0:T(8,128)(2,1)} %bitcast.8, bf16[1,8192]{1,0:T(2,128)(2,1)} %broadcast_in_dim.6.gain_ref, bf16[2048,512]{1,0:T(8,128)(2,1)} %key_ref.1, bf16[2048,512]{1,0:T(8,128)(2,1)} %value_ref.1, s32[8,8,128]{2,1,0:T(8,128)} %pad.4.table_ref), custom_call_target="tpu_custom_call" | custom-call | tf_op jit(solution)/shard_map/pallas_call | solution.py:376
  116.5 25.6 %shard_map.74 = bf16[256,4096]{1,0:T(8,128)(2,1)} custom-call(s32[8,8,128]{2,1,0:T(8,128)} %get-tuple-element.7.lists_ref, bf16[256,4096]{1,0:T(8,128)(2,1)} %bitcast.9, bf16[8,2,256,512]{3,2,1,0:T(8,128)(2,1)} %get-tuple-element.8.keys_ref.values_ref, bf16[8,2,256,512]{3,2,1,0:T(8,128)(2,1)} %get-tuple-element.8.keys_ref.values_ref), custom_call_target="tpu_custom_call" | custom-call | tf_op jit(solution)/shard_map/pallas_call | solution.py:106
  (1 shorter events, 0.0 us)
